TPU v7x, 32 devices: a whole 2x2x4 slice. The times are simulated.
32 devices in a mesh: dp: 2 (over x), orient: 16 (over z, y, core).
Axes of the slice: x: 2, y: 2, z: 4, core: 2. Of those that a mesh axis runs over, the one named last changes fastest.
Arguments:
- images: bfloat16 [384, 16384], P(('dp', 'orient')), may hold values from -80 to 80
- templates: bfloat16 [4096, 16384], P('orient'), as said below
- index: int32 [4096, 128], P('orient'), may hold values from 0 to 16383
- interp: float32 [4096, 128], P('orient'), may hold values from 0.25 to 1
- inv_noise: float32 [128, 128], replicated, may hold values from 0.5 to 2, as said below
Outputs:
- recon: float32 [16384, 128], P(('dp', 'orient'))
- recon_weight: float32 [16384, 128], P(('dp', 'orient'))
Inputs may be any that keep to these rules, and one draw needn't show every extreme that they name: `templates`: every entry has magnitude at most 18 / 128. `inv_noise`: every entry is 0.5, 1 or 2.
All inputs are finite; a program needn't handle non-finite values.
Results may differ from a plain program's by a relative error of at most 0.0029.
Values may be sent and summed in bfloat16 or wider, within the bound.
A program may use at most 128 MiB of HBM per device.

v0:
```python
import jax
import jax.numpy as jnp
from jax import lax
from jax.sharding import PartitionSpec as P


def shards(images, templates, index, interp, inv_noise):
    side = inv_noise.shape[0]
    count_tpl = templates.shape[0]
    noise_flat = inv_noise.reshape(-1)
    tpl_f = templates.astype(jnp.float32)
    weighted = (tpl_f * noise_flat[None, :]).astype(jnp.bfloat16)
    tnorm = 0.5 * jnp.sum(tpl_f * tpl_f * noise_flat[None, :], axis=1)
    gathered = lax.all_gather(images, "orient", axis=0, tiled=True)
    scores = (
        lax.dot_general(
            gathered, weighted, (((1,), (1,)), ((), ())), preferred_element_type=jnp.float32
        )
        - tnorm[None, :]
    )
    peak = lax.pmax(jnp.max(scores, axis=1), "orient")
    expo = jnp.exp(scores - peak[:, None])
    total = lax.psum(jnp.sum(expo, axis=1), "orient")
    posterior = expo / total[:, None]
    post_b = posterior.astype(jnp.bfloat16)
    mass = jnp.sum(posterior, axis=0)
    sums = lax.dot_general(
        post_b, gathered, (((0,), (0,)), ((), ())), preferred_element_type=jnp.float32
    )
    rows_idx = index.reshape(-1)
    data_rows = sums.reshape(count_tpl * side, side) * interp.reshape(-1, 1)
    data_vol = jnp.zeros((side * side, side), jnp.float32).at[rows_idx].add(data_rows)
    weight_rows = ((interp * mass[:, None])[:, :, None] * inv_noise[None, :, :]).reshape(
        count_tpl * side, side
    )
    weight_vol = jnp.zeros((side * side, side), jnp.float32).at[rows_idx].add(weight_rows)
    volume = jnp.concatenate([data_vol, weight_vol], axis=1)
    owned = lax.psum_scatter(volume, ("dp", "orient"), scatter_dimension=0, tiled=True)
    return (owned[:, :side], owned[:, side:])


def solution(mesh):
    placed = (
        P(("dp", "orient"), None),
        P("orient", None),
        P("orient", None),
        P("orient", None),
        P(),
    )
    return jax.shard_map(
        shards,
        mesh=mesh,
        in_specs=placed,
        out_specs=(P(("dp", "orient"), None), P(("dp", "orient"), None)),
        check_vma=False,
    )
```

profile of v0, /device:TPU:12, one launch (start us, length us, event | category | flops | bytes accessed | tf_op | source)
XLA Modules:
  0.0 775.7 jit_solution(3466400453175574872)
XLA Ops:
  7.2 0.0 copy-start.1
  7.2 0.0 all-gather.3.cloned.1.call-start
  7.2 0.7 all-gather.3.cloned.1.call-update
  7.9 0.0 reduce-scatter.2.cloned.1.call-start
  8.0 5.7 fusion.2
  13.6 1.0 compare_select_fusion
  14.7 70.0 %all-gather.3.cloned.1.call-done = bf16[16,12,16384]{2,1,0:T(8,128)(2,1)} async-done(((bf16[1,12,16384]{2,1,0:T(8,128)(2,1)}), bf16[16,12,16384]{2,1,0:T(8,128)(2,1)}) %all-gather.3.cloned.1.call-update) | async-done | bytes 6291472 | tf_op jit(solution)/shard_map/all_gather | solution.py:14
  84.7 8.8 %reshape.72 = bf16[192,16384]{1,0:T(8,128)(2,1)} reshape(bf16[16,12,16384]{2,1,0:T(8,128)(2,1)} %all-gather.3.cloned.1.call-done) | data formatting | bytes 12582912
  93.5 0.0 copy-done.1
  93.5 8.2 %fusion.22 = (f32[192]{0:T(256)S(1)}, f32[256,192]{0,1:T(8,128)S(1)}) fusion(f32[256]{0:T(256)S(1)} %broadcast_multiply_fusion, bf16[192,16384]{1,0:T(8,128)(2,1)} %reshape.72, bf16[256,16384]{1,0:T(8,128)(2,1)} %param.6, f32[16384]{0:T(1024)S(1)} %bitcast.14), kind=kOutput, calls=%fused_computation.28 | convolution fusion | flops 1623293696 | bytes 14944000 | tf_op jit(solution)/shard_map/dot_general | solution.py:16
  101.7 21.6 %pmax.7 = f32[192]{0:T(256)S(1)} all-reduce(f32[192]{0:T(256)S(1)} %get-tuple-element.4), channel_id=1, replica_groups=mesh['dp'=2,'orient'=16] {'orient'}, use_global_device_ids=true, to_apply=%region_2.0 | all-reduce | flops 192 | bytes 1536 | tf_op jit(solution)/shard_map/pmax | solution.py:21
  123.3 0.2 fusion.16
  123.5 28.1 %psum.7 = f32[192]{0:T(256)S(1)} all-reduce(f32[192]{0:T(256)S(1)} %fusion.16), channel_id=1, replica_groups=mesh['dp'=2,'orient'=16] {'orient'}, use_global_device_ids=true, to_apply=%region_4.0 | all-reduce | flops 192 | bytes 1536 | tf_op jit(solution)/shard_map/psum | solution.py:23
  151.5 11.0 %fusion.17 = f32[256,16384]{1,0:T(8,128)} fusion(bf16[192,16384]{1,0:T(8,128)(2,1)} %reshape.72, f32[256,192]{0,1:T(8,128)S(1)} %get-tuple-element.5, f32[192]{0:T(256)S(1)} %psum.7, f32[192]{0:T(256)S(1)} %pmax.7), kind=kOutput, calls=%fused_computation.23 | convolution fusion | flops 1610760192 | bytes 23266816 | tf_op jit(solution)/shard_map/dot_general | solution.py:27
  162.5 0.1 fusion.19
  162.6 0.0 copy-start
  162.7 18.1 %reshape.54 = f32[32768,128]{1,0:T(8,128)} reshape(f32[256,16384]{1,0:T(8,128)} %fusion.17) | data formatting | bytes 33554432 | tf_op jit(solution)/shard_map/reshape | solution.py:31
  180.7 0.0 copy-done
  180.7 0.1 multiply_bitcast_fusion
  180.8 8.5 %bitcast_multiply_fusion = f32[32768,128]{1,0:T(8,128)} fusion(f32[128,128]{1,0:T(8,128)S(1)} %copy-done.1, f32[32768]{0:T(1024)S(1)} %multiply_bitcast_fusion), kind=kLoop, calls=%fused_computation.8 | loop fusion | flops 4194304 | bytes 16973824 | tf_op jit(solution)/shard_map/mul | solution.py:33
  189.3 177.9 %scatter_custom_fusion.1 = f32[16384,128]{1,0:T(8,128)} fusion(s32[32768]{0:T(1024)S(1)} %bitcast.16, f32[32768,128]{1,0:T(8,128)} %bitcast_multiply_fusion, f32[]{:T(128)} %constant.5.clone.1), kind=kCustom, calls=%fused_computation.14 | custom fusion | flops 4194304 | bytes 8389120 | tf_op jit(solution)/shard_map/scatter-add | solution.py:36
  367.2 194.9 %scatter_custom_fusion = f32[16384,128]{1,0:T(8,128)} fusion(s32[32768]{0:T(1024)S(1)} %bitcast.17, f32[32768,128]{1,0:T(8,128)} %reshape.54, f32[32768]{0:T(1024)S(1)} %bitcast.11, f32[]{:T(128)} %constant.5.clone.1), kind=kCustom, calls=%fused_computation.9 | custom fusion | flops 8388608 | bytes 25296900 | tf_op jit(solution)/shard_map/scatter-add | solution.py:32
  562.0 11.3 %pad_maximum_fusion = f32[16384,256]{1,0:T(8,128)} fusion(f32[16384,128]{1,0:T(8,128)} %scatter_custom_fusion.1, f32[16384,128]{1,0:T(8,128)} %scatter_custom_fusion), kind=kLoop, calls=%fused_computation.7 | loop fusion | flops 4194304 | bytes 33554432 | tf_op jit(solution)/shard_map/concatenate | solution.py:37
  573.3 0.0 reduce-scatter.2.cloned.1.call-update
  573.4 193.7 %reduce-scatter.2.cloned.1.call-done = f32[512,256]{1,0:T(8,128)} async-done(((f32[16384,256]{1,0:T(8,128)}), f32[512,256]{1,0:T(8,128)}) %reduce-scatter.2.cloned.1.call-update) | async-done | bytes 524304 | tf_op jit(solution)/shard_map/reduce_scatter | solution.py:38
  767.0 1.9 fusion.21
  (1 shorter events, 0.0 us)
Async XLA Ops:
  7.2 86.3 %copy-start.1 = (f32[128,128]{1,0:T(8,128)S(1)}, f32[128,128]{1,0:T(8,128)}, u32[]{:S(2)}) copy-start(f32[128,128]{1,0:T(8,128)} %param.9) | copy-start | bytes 196612
  7.2 77.5 %all-gather.3.cloned.1.call-start = ((), (), s32[]{:S(2)}) async-start(), calls=%async_computation.2 | async-start | bytes 8912896 | tf_op jit(solution)/shard_map/all_gather | solution.py:14
  7.9 759.1 %reduce-scatter.2.cloned.1.call-start = ((), (), s32[]{:S(2)}) async-start(), calls=%async_computation.1 | async-start | bytes 17301504 | tf_op jit(solution)/shard_map/reduce_scatter | solution.py:38
  162.6 18.1 %copy-start = (f32[256,128]{1,0:T(8,128)S(1)}, f32[256,128]{1,0:T(8,128)}, u32[]{:S(2)}) copy-start(f32[256,128]{1,0:T(8,128)} %param.8) | copy-start | bytes 393220
Sparse Core Ops, SparseCore 0:
  10.2 74.4 all-gather.2
  573.5 193.4 reduce-scatter.1
where the time goes:
time: 778 us; the launch traced here: 776 us
  other arithmetic  400 us (51%)
  waiting for transfers between devices  264 us (34%)
  blocking collectives  49.7 us (6%)
  local copies, waits for them, and re-layouts  28.7 us (4%)
  matrix products  19.2 us (2%)
  between operations  14.1 us (2%)
    scatter-add x1, other arithmetic, shards(): jnp.zeros((side * side, side), jnp.float32).at[rows_idx].add(data_rows)  195 us
    reduce_scatter x1, waiting for transfers between devices, shards(): lax.psum_scatter(volume, ('dp', 'orient'), scatter_dimension=0, tiled=True)  194 us
    scatter-add x1, other arithmetic, shards(): jnp.zeros((side * side, side), jnp.float32).at[rows_idx].add(weight_rows)  178 us
    all_gather x1, waiting for transfers between devices, shards(): gathered = lax.all_gather(images, 'orient', axis=0, tiled=True)  70 us
    psum x1, blocking collectives, shards(): total = lax.psum(jnp.sum(expo, axis=1), 'orient')  28.1 us
    pmax x1, blocking collectives, shards(): peak = lax.pmax(jnp.max(scores, axis=1), 'orient')  21.6 us
    reshape x1, local copies, waits for them, and re-layouts, shards(): data_rows = sums.reshape(count_tpl * side, side) * interp.reshape(-1, 1)  18.1 us
  transfers between devices with their start and end apart: 2, of which 2 were waited for; matrix products, arithmetic and copies ran while one was open for 1% of the time, Pallas kernels for 0%

commit v1 on v0

v1 whole, which is shorter than its diff:
```python
import functools

import jax
import jax.numpy as jnp
from jax import lax
from jax.experimental import pallas as pl
from jax.experimental.pallas import tpu as pltpu
from jax.sharding import PartitionSpec as P

LANES = 128
ROWS_STEP = 8
ACCS = 4
UNROLL = 16
VMEM_LIMIT = 56 * 2**20


def data_kernel(post_ref, images_ref, interp_ref, idx_ref, out_ref, rows_ref, *accs):
    step = pl.program_id(0)
    count, side = post_ref.shape[0], out_ref.shape[1]
    volume_rows = out_ref.shape[0]
    every = (out_ref,) + accs

    @pl.when(step == 0)
    def _():
        @pl.loop(0, volume_rows // 64)
        def _(c):
            rows = pl.ds(pl.multiple_of(c * 64, 64), 64)
            for acc in every:
                acc[rows, :] = jnp.zeros((64, side), jnp.float32)

    for j in range(ROWS_STEP):
        block = jnp.dot(
            post_ref[...],
            images_ref[:, j * side : (j + 1) * side],
            preferred_element_type=jnp.float32,
        )
        rows_ref[j * count : (j + 1) * count, :] = block * interp_ref[0, :, j : j + 1]

    @pl.loop(0, ROWS_STEP * count // UNROLL)
    def _(g):
        base = pl.multiple_of(g * UNROLL, UNROLL)
        for k in range(UNROLL):
            acc = every[k % len(every)]
            v = idx_ref[0, 0, base + k]
            acc[pl.ds(v, 1), :] += rows_ref[pl.ds(base + k, 1), :]

    @pl.when(step == pl.num_programs(0) - 1)
    def _():
        @pl.loop(0, volume_rows // 64)
        def _(c):
            rows = pl.ds(pl.multiple_of(c * 64, 64), 64)
            total = every[0][rows, :]
            for acc in accs:
                total = total + acc[rows, :]
            out_ref[rows, :] = total


def insert_data(post, gathered, interp_t, index_t, volume_rows):
    count, images = post.shape
    side = interp_t.shape[0]
    steps = side // ROWS_STEP
    interp_b = interp_t.reshape(steps, ROWS_STEP, count).transpose(0, 2, 1)
    index_b = index_t.reshape(steps, 1, ROWS_STEP * count)
    return pl.pallas_call(
        data_kernel,
        grid=(steps,),
        out_shape=jax.ShapeDtypeStruct((volume_rows, side), jnp.float32),
        in_specs=[
            pl.BlockSpec((count, images), lambda i: (0, 0)),
            pl.BlockSpec((images, ROWS_STEP * side), lambda i: (0, i)),
            pl.BlockSpec((1, count, ROWS_STEP), lambda i: (i, 0, 0)),
            pl.BlockSpec(
                (1, 1, ROWS_STEP * count), lambda i: (i, 0, 0), memory_space=pltpu.SMEM
            ),
        ],
        out_specs=pl.BlockSpec(
            (volume_rows, side), lambda i: (0, 0), pipeline_mode=pl.Buffered(1)
        ),
        scratch_shapes=[pltpu.VMEM((ROWS_STEP * count, side), jnp.float32)]
        + [pltpu.VMEM((volume_rows, side), jnp.float32)] * (ACCS - 1),
        compiler_params=pltpu.CompilerParams(vmem_limit_bytes=VMEM_LIMIT),
        cost_estimate=pl.CostEstimate(
            flops=200_000_000_000, bytes_accessed=200_000_000, transcendentals=0
        ),
    )(post, gathered, interp_b, index_b)


def split(value):
    high = value.astype(jnp.bfloat16)
    return high, (value - high.astype(jnp.float32)).astype(jnp.bfloat16)


def weight_kernel(idx_ref, interp_ref, mass_ref, noise_ref, out_ref, grid_ref):
    step = pl.program_id(0)
    count = idx_ref.shape[1]
    side = noise_ref.shape[0]
    high_rows = out_ref.shape[0] // LANES
    nt = (((1,), (1,)), ((), ()))
    iota_high = lax.broadcasted_iota(jnp.int32, (high_rows, count), 0)
    iota_low = lax.broadcasted_iota(jnp.int32, (LANES, count), 0)
    one, zero = jnp.float32(1), jnp.float32(0)
    for j in range(ROWS_STEP):
        voxel = idx_ref[j : j + 1, :]
        weight = interp_ref[j : j + 1, :] * mass_ref[...]
        w_high = weight.astype(jnp.bfloat16).astype(jnp.float32)
        w_low = weight - w_high
        hot = jnp.where(iota_high == (voxel >> 7), one, zero).astype(jnp.bfloat16)
        low = iota_low == (voxel & (LANES - 1))
        part = lax.dot_general(
            hot,
            jnp.where(low, w_high, zero).astype(jnp.bfloat16),
            nt,
            preferred_element_type=jnp.float32,
        ) + lax.dot_general(
            hot,
            jnp.where(low, w_low, zero).astype(jnp.bfloat16),
            nt,
            preferred_element_type=jnp.float32,
        )
        row = pl.multiple_of((step * ROWS_STEP + j) * high_rows, 8)
        grid_ref[pl.ds(row, high_rows), :] = part

    @pl.when(step == pl.num_programs(0) - 1)
    def _():
        noise = noise_ref[...].astype(jnp.bfloat16)
        tn = (((0,), (0,)), ((), ()))

        @pl.loop(0, high_rows)
        def _(h):
            high, low = split(grid_ref[pl.ds(h, side, stride=high_rows), :])
            out_ref[pl.ds(pl.multiple_of(h * LANES, LANES), LANES), :] = lax.dot_general(
                high, noise, tn, preferred_element_type=jnp.float32
            ) + lax.dot_general(low, noise, tn, preferred_element_type=jnp.float32)


def insert_weights(index_t, interp_t, mass, inv_noise, volume_rows):
    side, count = index_t.shape
    return pl.pallas_call(
        weight_kernel,
        grid=(side // ROWS_STEP,),
        out_shape=jax.ShapeDtypeStruct((volume_rows, side), jnp.float32),
        in_specs=[
            pl.BlockSpec((ROWS_STEP, count), lambda i: (i, 0)),
            pl.BlockSpec((ROWS_STEP, count), lambda i: (i, 0)),
            pl.BlockSpec((1, count), lambda i: (0, 0)),
            pl.BlockSpec((side, side), lambda i: (0, 0)),
        ],
        out_specs=pl.BlockSpec(
            (volume_rows, side), lambda i: (0, 0), pipeline_mode=pl.Buffered(1)
        ),
        scratch_shapes=[pltpu.VMEM((volume_rows, side), jnp.float32)],
        compiler_params=pltpu.CompilerParams(vmem_limit_bytes=VMEM_LIMIT),
        cost_estimate=pl.CostEstimate(
            flops=20_000_000_000, bytes_accessed=20_000_000, transcendentals=0
        ),
    )(index_t, interp_t, mass.reshape(1, count), inv_noise)


def shards(images, templates, index, interp, inv_noise):
    side = inv_noise.shape[0]
    volume_rows = side * side
    noise_flat = inv_noise.reshape(-1)
    index_t, interp_t = index.T, interp.T
    gathered = lax.all_gather(images, "orient", axis=0, tiled=True)
    tpl_f = templates.astype(jnp.float32)
    weighted = (tpl_f * noise_flat[None, :]).astype(jnp.bfloat16)
    tnorm = 0.5 * jnp.sum(tpl_f * tpl_f * noise_flat[None, :], axis=1)
    scores = (
        lax.dot_general(
            weighted, gathered, (((1,), (1,)), ((), ())), preferred_element_type=jnp.float32
        )
        - tnorm[:, None]
    )
    peak_own = jnp.max(scores, axis=0)
    expo = jnp.exp(scores - peak_own[None, :])
    stats = lax.all_gather(jnp.stack([peak_own, jnp.sum(expo, axis=0)]), "orient", axis=0)
    peak = jnp.max(stats[:, 0], axis=0)
    total = jnp.sum(stats[:, 1] * jnp.exp(stats[:, 0] - peak[None, :]), axis=0)
    posterior = expo * (jnp.exp(peak_own - peak) / total)[None, :]
    mass = jnp.sum(posterior, axis=1)
    weight_vol = insert_weights(index_t, interp_t, mass, inv_noise, volume_rows)
    weight_vol, post_b = lax.optimization_barrier(
        (weight_vol, posterior.astype(jnp.bfloat16))
    )
    weight_own = lax.psum_scatter(
        weight_vol, ("dp", "orient"), scatter_dimension=0, tiled=True
    )
    data_vol = insert_data(post_b, gathered, interp_t, index_t, volume_rows)
    data_own = lax.psum_scatter(data_vol, ("dp", "orient"), scatter_dimension=0, tiled=True)
    return data_own, weight_own


def solution(mesh):
    placed = (
        P(("dp", "orient"), None),
        P("orient", None),
        P("orient", None),
        P("orient", None),
        P(),
    )
    return jax.shard_map(
        shards,
        mesh=mesh,
        in_specs=placed,
        out_specs=(P(("dp", "orient"), None), P(("dp", "orient"), None)),
        check_vma=False,
    )
```

time: 778 us -> 537 us (0.69)
  the two profiles are of different devices: /device:TPU:12 before, /device:TPU:0 now
where the time goes in v1:
time: 537 us; the launch traced here: 536 us
  waiting for transfers between devices  364 us (68%)
  Pallas kernels  111 us (21%)
  blocking collectives  18.8 us (4%)
  between operations  13.8 us (3%)
  local copies, waits for them, and re-layouts  13.6 us (3%)
  matrix products  7.53 us (1%)
  other arithmetic  7.08 us (1%)
    reduce_scatter x1, waiting for transfers between devices, shards(): lax.psum_scatter(weight_vol, ('dp', 'orient'), scatter_dimension=0, tiled...  147 us
    reduce_scatter x1, waiting for transfers between devices, shards(): lax.psum_scatter(data_vol, ('dp', 'orient'), scatter_dimension=0, tiled=T...  146 us
    all_gather x1, waiting for transfers between devices, shards(): gathered = lax.all_gather(images, 'orient', axis=0, tiled=True)  69.3 us
    pallas_call x1, Pallas kernels, insert_data(): pl.pallas_call(data_kernel, grid=(steps,), out_shape=jax.ShapeDtypeStruct...  64.7 us
    pallas_call x1, Pallas kernels, insert_weights(): pl.pallas_call(weight_kernel, grid=(side // ROWS_STEP,), out_shape=jax.Sh...  46.6 us
    all_gather x1, blocking collectives, shards(): lax.all_gather(jnp.stack([peak_own, jnp.sum(expo, axis=0)]), 'orient', ax...  18.8 us
    unnamed x9, local copies, waits for them, and re-layouts  10.9 us
  transfers between devices with their start and end apart: 3, of which 3 were waited for; matrix products, arithmetic and copies ran while one was open for 2% of the time, Pallas kernels for 0%

profile of v1, /device:TPU:0, one launch (start us, length us, event | category | flops | bytes accessed | tf_op | source)
XLA Modules:
  0.0 536.0 jit_solution(14750241148320152986)
XLA Ops:
  7.2 0.0 all-gather.5.cloned.1.call-start
  7.2 0.7 all-gather.5.cloned.1.call-update
  7.9 0.0 reduce-scatter.3.cloned.1.call-start
  7.9 1.0 copy.17
  8.9 0.0 copy-start
  9.0 1.0 copy.16
  10.0 0.0 copy-start.1
  10.0 0.8 reshape.30.idx_ref
  10.8 2.0 copy.20
  12.8 5.7 %fusion.2 = f32[256]{0:T(256)S(1)} fusion(bf16[256,16384]{1,0:T(8,128)(2,1)} %param.6, f32[16384]{0:T(1024)} %bitcast.31), kind=kLoop, calls=%fused_computation.4 | loop fusion | flops 16776960 | bytes 8455168 | tf_op jit(solution)/shard_map/reduce_sum | solution.py:167
  18.4 0.0 copy-start.2
  18.5 69.3 %all-gather.5.cloned.1.call-done = bf16[16,12,16384]{2,1,0:T(8,128)(2,1)} async-done(((bf16[1,12,16384]{2,1,0:T(8,128)(2,1)}), bf16[16,12,16384]{2,1,0:T(8,128)(2,1)}) %all-gather.5.cloned.1.call-update) | async-done | bytes 6291472 | tf_op jit(solution)/shard_map/all_gather | solution.py:164
  87.8 8.8 %reshape.33.images_ref = bf16[192,16384]{1,0:T(8,128)(2,1)} reshape(bf16[16,12,16384]{2,1,0:T(8,128)(2,1)} %all-gather.5.cloned.1.call-done) | data formatting | bytes 12582912
  96.6 0.0 copy-done
  96.6 0.0 copy-done.1
  96.6 0.0 copy-done.2
  96.6 7.5 %fusion.13 = (f32[192]{0:T(256)S(1)}, f32[256,192]{1,0:T(8,128)S(1)}) fusion(f32[256]{0:T(256)S(1)} %broadcast_multiply_fusion, bf16[192,16384]{1,0:T(8,128)(2,1)} %reshape.33.images_ref, bf16[256,16384]{1,0:T(8,128)(2,1)} %param.6, f32[16384]{0:T(1024)S(1)} %bitcast.32), kind=kOutput, calls=%fused_computation.21 | convolution fusion | flops 1623293696 | bytes 14944000 | tf_op jit(solution)/shard_map/dot_general | solution.py:169
  104.1 0.1 fusion.9
  104.2 18.8 %all-gather.2 = f32[16,2,192]{2,1,0:T(2,128)S(1)} all-gather(f32[1,2,192]{2,1,0:T(2,128)S(1)} %maximum_bitcast_fusion), channel_id=2, replica_groups=mesh['dp'=2,'orient'=16] {'orient'}, dimensions={0}, use_global_device_ids=true | all-gather | bytes 26112 | tf_op jit(solution)/shard_map/all_gather | solution.py:176
  123.1 1.2 multiply_convert_fusion
  124.4 46.6 %shard_map.68 = f32[16384,128]{1,0:T(8,128)} custom-call(s32[128,256]{1,0:T(8,128)} %bitcast.30, f32[128,256]{1,0:T(8,128)} %bitcast.27, f32[1,256]{1,0:T(1,128)} %bitcast.35, f32[128,128]{1,0:T(8,128)} %noise_ref.1), custom_call_target="tpu_custom_call" | custom-call | flops 20000000000 | bytes 20000000 | tf_op jit(solution)/shard_map/pallas_call | solution.py:138
  171.0 64.7 %shard_map.69 = f32[16384,128]{1,0:T(8,128)} custom-call(bf16[256,192]{1,0:T(8,128)(2,1)} %get-tuple-element.4.post_ref, bf16[192,16384]{1,0:T(8,128)(2,1)} %reshape.33.images_ref, f32[16,256,8]{2,1,0:T(8,128)} %bitcast.25, s32[16,1,2048]{2,1,0:T(1,128)} %reshape.30.idx_ref), custom_call_target="tpu_custom_call" | custom-call | flops 199999995904 | bytes 200000000 | tf_op jit(solution)/shard_map/pallas_call | solution.py:64
  235.7 0.0 reduce-scatter.3.cloned.1.call-update
  235.7 0.0 reduce-scatter.5.cloned.1.call-start
  235.8 0.7 reduce-scatter.5.cloned.1.call-update
  236.5 145.5 %reduce-scatter.3.cloned.1.call-done = f32[512,128]{1,0:T(8,128)} async-done(((f32[16384,128]{1,0:T(8,128)}), f32[512,128]{1,0:T(8,128)}) %reduce-scatter.3.cloned.1.call-update) | async-done | bytes 262160 | tf_op jit(solution)/shard_map/reduce_scatter | solution.py:189
  382.0 147.5 %reduce-scatter.5.cloned.1.call-done = f32[512,128]{1,0:T(8,128)} async-done(((f32[16384,128]{1,0:T(8,128)}), f32[512,128]{1,0:T(8,128)}) %reduce-scatter.5.cloned.1.call-update) | async-done | bytes 262160 | tf_op jit(solution)/shard_map/reduce_scatter | solution.py:185
  (5 shorter events, 0.1 us)
Async XLA Ops:
  7.2 80.6 %all-gather.5.cloned.1.call-start = ((), (), s32[]{:S(2)}) async-start(), calls=%async_computation.4 | async-start | bytes 8912896 | tf_op jit(solution)/shard_map/all_gather | solution.py:164
  7.9 374.1 %reduce-scatter.3.cloned.1.call-start = ((), (), s32[]{:S(2)}) async-start(), calls=%async_computation.2 | async-start | bytes 8650752 | tf_op jit(solution)/shard_map/reduce_scatter | solution.py:189
  8.9 87.7 %copy-start = (f32[256,128]{0,1:T(8,128)}, f32[256,128]{0,1:T(8,128)S(1)}, u32[]{:S(2)}) copy-start(f32[256,128]{0,1:T(8,128)S(1)} %copy.17) | copy-start | bytes 393220
  10.0 86.6 %copy-start.1 = (s32[256,128]{0,1:T(8,128)}, s32[256,128]{0,1:T(8,128)S(1)}, u32[]{:S(2)}) copy-start(s32[256,128]{0,1:T(8,128)S(1)} %copy.16) | copy-start | bytes 393220
  18.4 78.2 %copy-start.2 = (f32[128,128]{1,0:T(8,128)S(1)}, f32[128,128]{1,0:T(8,128)}, u32[]{:S(2)}) copy-start(f32[128,128]{1,0:T(8,128)} %noise_ref.1) | copy-start | bytes 196612
  235.7 293.8 %reduce-scatter.5.cloned.1.call-start = ((), (), s32[]{:S(2)}) async-start(), calls=%async_computation.3 | async-start | bytes 8650752 | tf_op jit(solution)/shard_map/reduce_scatter | solution.py:185
Sparse Core Ops, SparseCore 0:
  10.2 77.5 all-gather.4
  235.9 146.1 reduce-scatter.2
  384.9 144.5 reduce-scatter.4

commit v2 on v1

v2 whole, which is shorter than its diff:
```python
import functools

import jax
import jax.numpy as jnp
from jax import lax
from jax.experimental import pallas as pl
from jax.experimental.pallas import tpu as pltpu
from jax.sharding import PartitionSpec as P

LANES = 128
ROWS_STEP = 8
ACCS = 4
UNROLL = 16
LOW_BITS = 5
LOW = 1 << LOW_BITS
VMEM_LIMIT = 56 * 2**20


def data_kernel(post_ref, images_ref, interp_ref, idx_ref, out_ref, rows_ref, *accs):
    step = pl.program_id(0)
    count, side = post_ref.shape[0], out_ref.shape[1]
    volume_rows = out_ref.shape[0]

    @pl.when(step == 0)
    def _():
        @pl.loop(0, volume_rows // 64)
        def _(c):
            rows = pl.ds(pl.multiple_of(c * 64, 64), 64)
            for acc in accs:
                acc[rows, :] = jnp.zeros((64, side), jnp.float32)

    for j in range(ROWS_STEP):
        block = jnp.dot(
            post_ref[...],
            images_ref[:, j * side : (j + 1) * side],
            preferred_element_type=jnp.float32,
        )
        rows_ref[j * count : (j + 1) * count, :] = block * interp_ref[0, :, j : j + 1]

    @pl.loop(0, ROWS_STEP * count // UNROLL)
    def _(g):
        base = pl.multiple_of(g * UNROLL, UNROLL)
        for k in range(UNROLL):
            acc = accs[k % ACCS]
            v = idx_ref[0, 0, base + k]
            acc[pl.ds(v, 1), :] += rows_ref[pl.ds(base + k, 1), :]

    @pl.when(step == pl.num_programs(0) - 1)
    def _():
        @pl.loop(0, volume_rows // 64)
        def _(c):
            rows = pl.ds(pl.multiple_of(c * 64, 64), 64)
            total = accs[0][rows, :]
            for acc in accs[1:]:
                total = total + acc[rows, :]
            out_ref[rows, :] = total.astype(out_ref.dtype)


def insert_data(post, gathered, interp_t, index_t, volume_rows):
    count, images = post.shape
    side = interp_t.shape[0]
    steps = side // ROWS_STEP
    interp_b = interp_t.reshape(steps, ROWS_STEP, count).transpose(0, 2, 1)
    index_b = index_t.reshape(steps, 1, ROWS_STEP * count)
    return pl.pallas_call(
        data_kernel,
        grid=(steps,),
        out_shape=jax.ShapeDtypeStruct((volume_rows, side), jnp.bfloat16),
        in_specs=[
            pl.BlockSpec((count, images), lambda i: (0, 0)),
            pl.BlockSpec((images, ROWS_STEP * side), lambda i: (0, i)),
            pl.BlockSpec((1, count, ROWS_STEP), lambda i: (i, 0, 0)),
            pl.BlockSpec(
                (1, 1, ROWS_STEP * count), lambda i: (i, 0, 0), memory_space=pltpu.SMEM
            ),
        ],
        out_specs=pl.BlockSpec(
            (volume_rows, side), lambda i: (0, 0), pipeline_mode=pl.Buffered(1)
        ),
        scratch_shapes=[pltpu.VMEM((ROWS_STEP * count, side), jnp.float32)]
        + [pltpu.VMEM((volume_rows, side), jnp.float32)] * ACCS,
        compiler_params=pltpu.CompilerParams(vmem_limit_bytes=VMEM_LIMIT),
        cost_estimate=pl.CostEstimate(
            flops=200_000_000_000, bytes_accessed=200_000_000, transcendentals=0
        ),
    )(post, gathered, interp_b, index_b)


def reduce_kernel(
    groups, orient, blocks_ref, out_ref, mine, theirs, landed, own_sem, pair_send, pair_recv, send_sem, recv_sem
):
    half = orient // 2
    chips = groups * half
    group, place = lax.axis_index("dp"), lax.axis_index("orient")
    core = lax.rem(place, 2)
    me = group * half + lax.div(place, 2)
    partner = (group, place + 1 - 2 * core)
    mesh_ids = pl.DeviceIdType.MESH

    def device(chip):
        return (lax.div(chip, half), lax.rem(chip, half) * 2 + core)

    barrier = pltpu.get_barrier_semaphore()
    pl.semaphore_signal(barrier, inc=1, device_id=partner, device_id_type=mesh_ids)

    @pl.loop(1, chips)
    def _(s):
        pl.semaphore_signal(
            barrier,
            inc=1,
            device_id=device(lax.rem(me + s, chips)),
            device_id_type=mesh_ids,
        )

    pl.semaphore_wait(barrier, chips)

    def own_copy(s):
        return pltpu.make_async_copy(
            blocks_ref.at[lax.rem(me + s, chips), core], mine.at[s], own_sem.at[s]
        )

    def pair_copy(s):
        return pltpu.make_async_remote_copy(
            src_ref=blocks_ref.at[lax.rem(me + s, chips), 1 - core],
            dst_ref=theirs.at[s],
            send_sem=pair_send.at[s],
            recv_sem=pair_recv.at[s],
            device_id=partner,
            device_id_type=mesh_ids,
        )

    def chip_copy(s):
        return pltpu.make_async_remote_copy(
            src_ref=mine.at[s],
            dst_ref=landed.at[s],
            send_sem=send_sem.at[s],
            recv_sem=recv_sem.at[s],
            device_id=device(lax.rem(me + s, chips)),
            device_id_type=mesh_ids,
        )

    @pl.loop(1, chips + 1)
    def _(k):
        s = lax.rem(k, chips)
        own_copy(s).start()
        pair_copy(s).start()

    @pl.loop(1, chips)
    def _(s):
        own_copy(s).wait()
        pair_copy(s).wait()
        mine[s] = (mine[s].astype(jnp.float32) + theirs[s].astype(jnp.float32)).astype(
            mine.dtype
        )
        chip_copy(s).start()

    own_copy(0).wait()
    pair_copy(0).wait()
    out_ref[...] = mine[0].astype(jnp.float32) + theirs[0].astype(jnp.float32)

    @pl.loop(1, chips)
    def _(s):
        chip_copy(s).wait()
        out_ref[...] += landed[s].astype(jnp.float32)


def reduce_rows(volume, groups, orient):
    chips = groups * orient // 2
    rows, side = volume.shape[0] // (2 * chips), volume.shape[1]
    return pl.pallas_call(
        functools.partial(reduce_kernel, groups, orient),
        out_shape=jax.ShapeDtypeStruct((rows, side), jnp.float32),
        in_specs=[pl.BlockSpec(memory_space=pl.ANY)],
        out_specs=pl.BlockSpec(memory_space=pltpu.VMEM),
        scratch_shapes=[pltpu.VMEM((chips, rows, side), volume.dtype)] * 3
        + [pltpu.SemaphoreType.DMA((chips,))] * 5,
        compiler_params=pltpu.CompilerParams(
            collective_id=0, has_side_effects=True, vmem_limit_bytes=24 * 2**20
        ),
    )(volume.reshape(chips, 2, rows, side))


def split(value):
    high = value.astype(jnp.bfloat16)
    return high, (value - high.astype(jnp.float32)).astype(jnp.bfloat16)


def weight_kernel(local_ref, weight_ref, noise_ref, out_ref, grid_ref):
    step = pl.program_id(0)
    count = local_ref.shape[1]
    side = noise_ref.shape[0]
    high_rows = grid_ref.shape[0] // side
    nt = (((1,), (1,)), ((), ()))
    iota_high = lax.broadcasted_iota(jnp.int32, (high_rows, count), 0)
    iota_low = lax.broadcasted_iota(jnp.int32, (LOW, count), 0)
    one, zero = jnp.float32(1), jnp.float32(0)
    for j in range(ROWS_STEP):
        local = local_ref[j : j + 1, :]
        hot = jnp.where(iota_high == (local >> LOW_BITS), one, zero)
        low = jnp.where(iota_low == (local & (LOW - 1)), weight_ref[j : j + 1, :], zero)
        part = lax.dot_general(
            hot.astype(jnp.bfloat16),
            low.astype(jnp.bfloat16),
            nt,
            preferred_element_type=jnp.float32,
        )
        row = pl.multiple_of((step * ROWS_STEP + j) * high_rows, 8)
        grid_ref[pl.ds(row, high_rows), :LOW] = part

    @pl.when(step == pl.num_programs(0) - 1)
    def _():
        noise = noise_ref[...].astype(jnp.bfloat16)
        tn = (((0,), (0,)), ((), ()))
        for h in range(out_ref.shape[0] // LOW):
            high, low = split(grid_ref[pl.ds(h, side, stride=high_rows), :])
            block = lax.dot_general(
                high, noise, tn, preferred_element_type=jnp.float32
            ) + lax.dot_general(low, noise, tn, preferred_element_type=jnp.float32)
            out_ref[h * LOW : (h + 1) * LOW, :] = block[:LOW]


def own_weights(local_t, weight_t, inv_noise, rows):
    side, count = local_t.shape
    high_rows = max(8, rows // LOW)
    return pl.pallas_call(
        weight_kernel,
        grid=(side // ROWS_STEP,),
        out_shape=jax.ShapeDtypeStruct((rows, side), jnp.float32),
        in_specs=[
            pl.BlockSpec((ROWS_STEP, count), lambda i: (i, 0)),
            pl.BlockSpec((ROWS_STEP, count), lambda i: (i, 0)),
            pl.BlockSpec((side, side), lambda i: (0, 0)),
        ],
        out_specs=pl.BlockSpec((rows, side), lambda i: (0, 0)),
        scratch_shapes=[pltpu.VMEM((side * high_rows, LANES), jnp.float32)],
        compiler_params=pltpu.CompilerParams(vmem_limit_bytes=24 * 2**20),
        cost_estimate=pl.CostEstimate(
            flops=60_000_000_000, bytes_accessed=20_000_000, transcendentals=0
        ),
    )(local_t, weight_t, inv_noise)


def shards(groups, orient, images, templates, index, interp, inv_noise):
    side = inv_noise.shape[0]
    volume_rows = side * side
    noise_flat = inv_noise.reshape(-1)
    index_t, interp_t = index.T, interp.T
    gathered = lax.all_gather(images, "orient", axis=0, tiled=True)
    places = jnp.concatenate([index.astype(jnp.float32), interp], axis=1)
    gathered, places = lax.optimization_barrier((gathered, places))
    places_all = lax.all_gather(places, "orient", axis=0, tiled=True)
    tpl_f = templates.astype(jnp.float32)
    weighted = (tpl_f * noise_flat[None, :]).astype(jnp.bfloat16)
    tnorm = 0.5 * jnp.sum(tpl_f * tpl_f * noise_flat[None, :], axis=1)
    scores = (
        lax.dot_general(
            weighted, gathered, (((1,), (1,)), ((), ())), preferred_element_type=jnp.float32
        )
        - tnorm[:, None]
    )
    peak_own = jnp.max(scores, axis=0)
    expo = jnp.exp(scores - peak_own[None, :])
    stats = lax.all_gather(jnp.stack([peak_own, jnp.sum(expo, axis=0)]), "orient", axis=0)
    peak = jnp.max(stats[:, 0], axis=0)
    total = jnp.sum(stats[:, 1] * jnp.exp(stats[:, 0] - peak[None, :]), axis=0)
    posterior = expo * (jnp.exp(peak_own - peak) / total)[None, :]
    mass = jnp.sum(posterior, axis=1)
    data_vol = insert_data(
        posterior.astype(jnp.bfloat16), gathered, interp_t, index_t, volume_rows
    )
    rows = volume_rows // (groups * orient)
    first = (lax.axis_index("dp") * orient + lax.axis_index("orient")) * rows
    masses = lax.all_gather(mass, ("dp", "orient"), axis=0)
    mass_all = jnp.sum(masses.reshape(groups, -1), axis=0)
    weight_own = own_weights(
        places_all[:, :side].astype(jnp.int32).T - first,
        places_all[:, side:].T * mass_all[None, :],
        inv_noise,
        rows,
    )
    return reduce_rows(data_vol, groups, orient), weight_own


def solution(mesh):
    placed = (
        P(("dp", "orient"), None),
        P("orient", None),
        P("orient", None),
        P("orient", None),
        P(),
    )
    return jax.shard_map(
        functools.partial(shards, mesh.shape["dp"], mesh.shape["orient"]),
        mesh=mesh,
        in_specs=placed,
        out_specs=(P(("dp", "orient"), None), P(("dp", "orient"), None)),
        check_vma=False,
    )
```

time: 537 us -> 308 us (0.57)
  waiting for transfers between devices: 364 us -> 68.4 us
  blocking collectives: 18.8 us -> 66 us
  Pallas kernels: 111 us -> 122 us
    reduce_scatter x2 -> x0, waiting for transfers between devices: 293 us -> none  [the longest x1 147 us: shards(): lax.psum_scatter(weight_vol, ('dp', 'orient'), scatter_dimension=0, tiled...]
    all_gather x0 -> x1, blocking collectives: none -> 47.2 us  [shards(): masses = lax.all_gather(mass, ('dp', 'orient'), axis=0)]
    pallas_call x1 -> x2, Pallas kernels: 46.6 us -> 58.8 us  [the longest x1 46.7 us: reduce_rows(): pl.pallas_call(functools.partial(reduce_kernel, groups, orient), out_shap...]
    optimization_barrier x0 -> x1, local copies, waits for them, and re-layouts: none -> 8.78 us  [shards(): gathered, places = lax.optimization_barrier((gathered, places))]
    unnamed x9 -> x11, local copies, waits for them, and re-layouts: 10.9 us -> 4.9 us
  transfers between devices with their start and end apart: 3 -> 2, of which waited for: 3 -> 1; matrix products, arithmetic and copies ran while one was open for 2% -> 4% of each run, Pallas kernels for 0% -> 36%
where the time goes in v2:
time: 308 us; the launch traced here: 307 us
  Pallas kernels  122 us (40%)
  waiting for transfers between devices  68.4 us (22%)
  blocking collectives  66 us (21%)
  local copies, waits for them, and re-layouts  17.4 us (6%)
  between operations  14.2 us (5%)
  other arithmetic  11.6 us (4%)
  matrix products  7.53 us (2%)
    all_gather x1, waiting for transfers between devices, shards(): gathered = lax.all_gather(images, 'orient', axis=0, tiled=True)  67.7 us
    pallas_call x1, Pallas kernels, insert_data(): pl.pallas_call(data_kernel, grid=(steps,), out_shape=jax.ShapeDtypeStruct...  63.5 us
    all_gather x1, blocking collectives, shards(): masses = lax.all_gather(mass, ('dp', 'orient'), axis=0)  47.2 us
    pallas_call x1, Pallas kernels, reduce_rows(): pl.pallas_call(functools.partial(reduce_kernel, groups, orient), out_shap...  46.7 us
    all_gather x1, blocking collectives, shards(): lax.all_gather(jnp.stack([peak_own, jnp.sum(expo, axis=0)]), 'orient', ax...  18.8 us
    pallas_call x1, Pallas kernels, own_weights(): pl.pallas_call(weight_kernel, grid=(side // ROWS_STEP,), out_shape=jax.Sh...  12 us
    optimization_barrier x1, local copies, waits for them, and re-layouts, shards(): gathered, places = lax.optimization_barrier((gathered, places))  8.78 us
    dot_general x1, matrix products, shards(): lax.dot_general(weighted, gathered, (((1,), (1,)), ((), ())), preferred_e...  7.53 us
  transfers between devices with their start and end apart: 2, of which 1 were waited for; matrix products, arithmetic and copies ran while one was open for 4% of the time, Pallas kernels for 36%

profile of v2, /device:TPU:0, one launch (start us, length us, event | category | flops | bytes accessed | tf_op | source)
XLA Modules:
  0.0 307.5 jit_solution(5186639506116071642)
XLA Ops:
  7.2 0.0 all-gather.10.cloned.1.call-start
  7.2 0.7 all-gather.10.cloned.1.call-update
  7.9 0.0 all-gather.8.cloned.1.call-start
  7.9 1.0 copy.20
  9.0 1.0 copy.19
  10.0 1.9 copy.24
  11.9 1.0 copy.25
  12.9 0.8 reshape.33.idx_ref
  13.7 0.7 pad_maximum_fusion
  14.4 5.7 %fusion.2 = f32[256]{0:T(256)S(1)} fusion(bf16[256,16384]{1,0:T(8,128)(2,1)} %param.6, f32[16384]{0:T(1024)} %bitcast.31), kind=kLoop, calls=%fused_computation.4 | loop fusion | flops 16776960 | bytes 8455168 | tf_op jit(solution)/shard_map/reduce_sum | solution.py:254
  20.1 0.0 copy-start.1
  20.1 67.7 %all-gather.10.cloned.1.call-done = bf16[16,12,16384]{2,1,0:T(8,128)(2,1)} async-done(((bf16[1,12,16384]{2,1,0:T(8,128)(2,1)}), bf16[16,12,16384]{2,1,0:T(8,128)(2,1)}) %all-gather.10.cloned.1.call-update) | async-done | bytes 6291472 | tf_op jit(solution)/shard_map/all_gather | solution.py:248
  87.8 8.8 %reshape.40.images_ref = bf16[192,16384]{1,0:T(8,128)(2,1)} reshape(bf16[16,12,16384]{2,1,0:T(8,128)(2,1)} %all-gather.10.cloned.1.call-done) | data formatting | bytes 12582912 | tf_op jit(solution)/shard_map/optimization_barrier | solution.py:250
  96.6 0.0 copy-done.1
  96.6 7.5 %fusion.16 = (f32[192]{0:T(256)S(1)}, f32[256,192]{1,0:T(8,128)S(1)}) fusion(f32[256]{0:T(256)S(1)} %broadcast_multiply_fusion, bf16[192,16384]{1,0:T(8,128)(2,1)} %reshape.40.images_ref, bf16[256,16384]{1,0:T(8,128)(2,1)} %param.6, f32[16384]{0:T(1024)S(1)} %bitcast.32), kind=kOutput, calls=%fused_computation.27 | convolution fusion | flops 1623293696 | bytes 14944000 | tf_op jit(solution)/shard_map/dot_general | solution.py:256
  104.1 0.1 fusion.12
  104.2 18.8 %all-gather.3 = f32[16,2,192]{2,1,0:T(2,128)S(1)} all-gather(f32[1,2,192]{2,1,0:T(2,128)S(1)} %maximum_bitcast_fusion), channel_id=2, replica_groups=mesh['dp'=2,'orient'=16] {'orient'}, dimensions={0}, use_global_device_ids=true | all-gather | bytes 26112 | tf_op jit(solution)/shard_map/all_gather | solution.py:263
  123.1 1.3 multiply_reduce_fusion
  124.4 0.0 all-gather.8.cloned.1.call-update
  124.4 0.0 copy-start.3
  124.4 63.5 %shard_map.68 = bf16[16384,128]{1,0:T(8,128)(2,1)} custom-call(bf16[256,192]{1,0:T(8,128)(2,1)} %get-tuple-element.7.post_ref, bf16[192,16384]{1,0:T(8,128)(2,1)} %reshape.40.images_ref, f32[16,256,8]{2,1,0:T(8,128)} %bitcast.33, s32[16,1,2048]{2,1,0:T(1,128)} %reshape.33.idx_ref), custom_call_target="tpu_custom_call" | custom-call | flops 199999995904 | bytes 200000000 | tf_op jit(solution)/shard_map/pallas_call | solution.py:65
  187.9 0.0 copy-start
  187.9 2.2 copy-done
  190.1 0.0 copy-start.2
  190.1 46.7 %shard_map.69 = f32[512,128]{1,0:T(8,128)S(1)} custom-call(bf16[16,2,512,128]{3,2,1,0:T(8,128)(2,1)S(1)} %bitcast.30), custom_call_target="tpu_custom_call" | custom-call | tf_op jit(solution)/shard_map/pallas_call | solution.py:170
  236.8 0.0 copy-done.3
  236.9 47.2 %all-gather.4 = f32[32,1,256]{2,1,0:T(1,128)S(1)} all-gather(f32[1,1,256]{2,1,0:T(1,128)S(1)} %bitcast.38), channel_id=3, replica_groups=mesh['dp'=2,'orient'=16] {'dp','orient'}, dimensions={0}, use_global_device_ids=true | all-gather | bytes 33792 | tf_op jit(solution)/shard_map/all_gather | solution.py:273
  284.1 0.1 reduce.1
  284.2 0.0 all-gather.8.cloned.1.call-done
  284.2 1.8 fusion.8.local_ref
  286.1 1.8 fusion.6.weight_ref
  287.9 0.0 copy-done.2
  287.9 12.0 %shard_map.70 = f32[512,128]{1,0:T(8,128)} custom-call(s32[128,4096]{1,0:T(8,128)S(1)} %fusion.8.local_ref, f32[128,4096]{1,0:T(8,128)S(1)} %fusion.6.weight_ref, f32[128,128]{1,0:T(8,128)S(1)} %copy-done.2), custom_call_target="tpu_custom_call" | custom-call | flops 60000002048 | bytes 20000000 | tf_op jit(solution)/shard_map/pallas_call | solution.py:225
  300.0 0.7 copy.36
  (8 shorter events, 0.2 us)
Async XLA Ops:
  7.2 80.6 %all-gather.10.cloned.1.call-start = ((), (), s32[]{:S(2)}) async-start(), calls=%async_computation.1 | async-start | bytes 8912896 | tf_op jit(solution)/shard_map/all_gather | solution.py:248
  7.9 276.3 %all-gather.8.cloned.1.call-start = ((), (), s32[]{:S(2)}) async-start(), calls=%async_computation | async-start | bytes 4456448 | tf_op jit(solution)/shard_map/all_gather | solution.py:251
  20.1 76.5 %copy-start.1 = (f32[128,128]{1,0:T(8,128)S(1)}, f32[128,128]{1,0:T(8,128)}, u32[]{:S(2)}) copy-start(f32[128,128]{1,0:T(8,128)} %noise_ref.1) | copy-start | bytes 196612
  124.4 112.4 %copy-start.3 = (f32[256]{0:T(256)S(1)}, f32[256]{0:T(256)}, u32[]{:S(2)}) copy-start(f32[256]{0:T(256)} %get-tuple-element.6) | copy-start | bytes 3076
  187.9 2.2 copy-start
  190.1 97.8 %copy-start.2 = (f32[128,128]{1,0:T(8,128)S(1)}, f32[128,128]{1,0:T(8,128)}, u32[]{:S(2)}) copy-start(f32[128,128]{1,0:T(8,128)} %noise_ref.1) | copy-start | bytes 196612
Sparse Core Ops, SparseCore 0:
  10.2 77.5 all-gather.9
  124.5 50.3 all-gather.7

commit v3 on v2

--- a/solution.py
+++ b/solution.py
@@ -16,7 +16,8 @@
 VMEM_LIMIT = 56 * 2**20
 
 
-def data_kernel(post_ref, images_ref, interp_ref, idx_ref, out_ref, rows_ref, *accs):
+def data_kernel(post_ref, images_ref, interp_ref, idx_ref, out_ref, rows_ref, *more):
+    accs = (out_ref,) + more
     step = pl.program_id(0)
     count, side = post_ref.shape[0], out_ref.shape[1]
     volume_rows = out_ref.shape[0]
@@ -53,7 +54,7 @@
             total = accs[0][rows, :]
             for acc in accs[1:]:
                 total = total + acc[rows, :]
-            out_ref[rows, :] = total.astype(out_ref.dtype)
+            out_ref[rows, :] = total
 
 
 def insert_data(post, gathered, interp_t, index_t, volume_rows):
@@ -65,7 +66,7 @@
     return pl.pallas_call(
         data_kernel,
         grid=(steps,),
-        out_shape=jax.ShapeDtypeStruct((volume_rows, side), jnp.bfloat16),
+        out_shape=jax.ShapeDtypeStruct((volume_rows, side), jnp.float32),
         in_specs=[
             pl.BlockSpec((count, images), lambda i: (0, 0)),
             pl.BlockSpec((images, ROWS_STEP * side), lambda i: (0, i)),
@@ -78,7 +79,7 @@
             (volume_rows, side), lambda i: (0, 0), pipeline_mode=pl.Buffered(1)
         ),
         scratch_shapes=[pltpu.VMEM((ROWS_STEP * count, side), jnp.float32)]
-        + [pltpu.VMEM((volume_rows, side), jnp.float32)] * ACCS,
+        + [pltpu.VMEM((volume_rows, side), jnp.float32)] * (ACCS - 1),
         compiler_params=pltpu.CompilerParams(vmem_limit_bytes=VMEM_LIMIT),
         cost_estimate=pl.CostEstimate(
             flops=200_000_000_000, bytes_accessed=200_000_000, transcendentals=0
@@ -87,7 +88,24 @@
 
 
 def reduce_kernel(
-    groups, orient, blocks_ref, out_ref, mine, theirs, landed, own_sem, pair_send, pair_recv, send_sem, recv_sem
+    groups,
+    orient,
+    blocks_ref,
+    mass_ref,
+    out_ref,
+    masses_ref,
+    mine,
+    theirs,
+    ready,
+    landed,
+    masses,
+    own_sem,
+    pair_send,
+    pair_recv,
+    send_sem,
+    recv_sem,
+    mass_send,
+    mass_recv,
 ):
     half = orient // 2
     chips = groups * half
@@ -100,19 +118,34 @@
     def device(chip):
         return (lax.div(chip, half), lax.rem(chip, half) * 2 + core)
 
+    devices = 2 * chips
+    rank = group * orient + place
+
+    def ranked(d):
+        return (lax.div(d, orient), lax.rem(d, orient))
+
     barrier = pltpu.get_barrier_semaphore()
-    pl.semaphore_signal(barrier, inc=1, device_id=partner, device_id_type=mesh_ids)
-
-    @pl.loop(1, chips)
+
+    @pl.loop(1, devices)
     def _(s):
         pl.semaphore_signal(
             barrier,
             inc=1,
-            device_id=device(lax.rem(me + s, chips)),
+            device_id=ranked(lax.rem(rank + s, devices)),
             device_id_type=mesh_ids,
         )
 
-    pl.semaphore_wait(barrier, chips)
+    pl.semaphore_wait(barrier, devices - 1)
+
+    def mass_copy(s):
+        return pltpu.make_async_remote_copy(
+            src_ref=mass_ref,
+            dst_ref=masses.at[s],
+            send_sem=mass_send.at[s],
+            recv_sem=mass_recv.at[s],
+            device_id=ranked(lax.rem(rank + s, devices)),
+            device_id_type=mesh_ids,
+        )
 
     def own_copy(s):
         return pltpu.make_async_copy(
@@ -131,7 +164,7 @@
 
     def chip_copy(s):
         return pltpu.make_async_remote_copy(
-            src_ref=mine.at[s],
+            src_ref=ready.at[s],
             dst_ref=landed.at[s],
             send_sem=send_sem.at[s],
             recv_sem=recv_sem.at[s],
@@ -145,18 +178,26 @@
         own_copy(s).start()
         pair_copy(s).start()
 
+    @pl.loop(1, devices)
+    def _(s):
+        mass_copy(s).start()
+
     @pl.loop(1, chips)
     def _(s):
         own_copy(s).wait()
         pair_copy(s).wait()
-        mine[s] = (mine[s].astype(jnp.float32) + theirs[s].astype(jnp.float32)).astype(
-            mine.dtype
-        )
+        ready[s] = (mine[s] + theirs[s]).astype(ready.dtype)
         chip_copy(s).start()
 
     own_copy(0).wait()
     pair_copy(0).wait()
-    out_ref[...] = mine[0].astype(jnp.float32) + theirs[0].astype(jnp.float32)
+    out_ref[...] = mine[0] + theirs[0]
+    masses_ref[rank] = mass_ref[...]
+
+    @pl.loop(1, devices)
+    def _(s):
+        mass_copy(s).wait()
+        masses_ref[lax.rem(rank + devices - s, devices)] = masses[s]
 
     @pl.loop(1, chips)
     def _(s):
@@ -164,20 +205,35 @@
         out_ref[...] += landed[s].astype(jnp.float32)
 
 
-def reduce_rows(volume, groups, orient):
+def reduce_rows(volume, mass, groups, orient):
     chips = groups * orient // 2
     rows, side = volume.shape[0] // (2 * chips), volume.shape[1]
+    parts = (chips, rows, side)
+    mass_rows = mass.reshape(-1, LANES)
+    masses = (2 * chips,) + mass_rows.shape
     return pl.pallas_call(
         functools.partial(reduce_kernel, groups, orient),
-        out_shape=jax.ShapeDtypeStruct((rows, side), jnp.float32),
-        in_specs=[pl.BlockSpec(memory_space=pl.ANY)],
-        out_specs=pl.BlockSpec(memory_space=pltpu.VMEM),
-        scratch_shapes=[pltpu.VMEM((chips, rows, side), volume.dtype)] * 3
-        + [pltpu.SemaphoreType.DMA((chips,))] * 5,
+        out_shape=(
+            jax.ShapeDtypeStruct((rows, side), jnp.float32),
+            jax.ShapeDtypeStruct(masses, jnp.float32),
+        ),
+        in_specs=[
+            pl.BlockSpec(memory_space=pl.ANY),
+            pl.BlockSpec(memory_space=pltpu.VMEM),
+        ],
+        out_specs=(
+            pl.BlockSpec(memory_space=pltpu.VMEM),
+            pl.BlockSpec(memory_space=pltpu.VMEM),
+        ),
+        scratch_shapes=[pltpu.VMEM(parts, jnp.float32)] * 2
+        + [pltpu.VMEM(parts, jnp.bfloat16)] * 2
+        + [pltpu.VMEM(masses, jnp.float32)]
+        + [pltpu.SemaphoreType.DMA((chips,))] * 5
+        + [pltpu.SemaphoreType.DMA((2 * chips,))] * 2,
         compiler_params=pltpu.CompilerParams(
-            collective_id=0, has_side_effects=True, vmem_limit_bytes=24 * 2**20
-        ),
-    )(volume.reshape(chips, 2, rows, side))
+            collective_id=0, has_side_effects=True, vmem_limit_bytes=32 * 2**20
+        ),
+    )(volume.reshape(chips, 2, rows, side), mass_rows)
 
 
 def split(value):
@@ -270,7 +326,7 @@
     )
     rows = volume_rows // (groups * orient)
     first = (lax.axis_index("dp") * orient + lax.axis_index("orient")) * rows
-    masses = lax.all_gather(mass, ("dp", "orient"), axis=0)
+    data_own, masses = reduce_rows(data_vol, mass, groups, orient)
     mass_all = jnp.sum(masses.reshape(groups, -1), axis=0)
     weight_own = own_weights(
         places_all[:, :side].astype(jnp.int32).T - first,
@@ -278,7 +334,7 @@
         inv_noise,
         rows,
     )
-    return reduce_rows(data_vol, groups, orient), weight_own
+    return data_own, weight_own
 
 
 def solution(mesh):

time: 308 us -> 267 us (0.87)
  the two profiles are of different devices: /device:TPU:0 before, /device:TPU:12 now
where the time goes in v3:
time: 267 us
  Pallas kernels  133 us (50%)
  waiting for transfers between devices  65.3 us (24%)
  local copies, waits for them, and re-layouts  18.6 us (7%)
  blocking collectives  16.5 us (6%)
  between operations  14.2 us (5%)
  other arithmetic  11 us (4%)
  matrix products  7.53 us (3%)
    pallas_call x1, Pallas kernels, insert_data(): pl.pallas_call(data_kernel, grid=(steps,), out_shape=jax.ShapeDtypeStruct...  64.7 us
    all_gather x1, waiting for transfers between devices, shards(): gathered = lax.all_gather(images, 'orient', axis=0, tiled=True)  64.6 us
    pallas_call x1, Pallas kernels, reduce_rows(): pl.pallas_call(functools.partial(reduce_kernel, groups, orient), out_shap...  56.6 us
    all_gather x1, blocking collectives, shards(): lax.all_gather(jnp.stack([peak_own, jnp.sum(expo, axis=0)]), 'orient', ax...  16.5 us
    pallas_call x1, Pallas kernels, own_weights(): pl.pallas_call(weight_kernel, grid=(side // ROWS_STEP,), out_shape=jax.Sh...  12 us
    optimization_barrier x1, local copies, waits for them, and re-layouts, shards(): gathered, places = lax.optimization_barrier((gathered, places))  8.78 us
    dot_general x1, matrix products, shards(): lax.dot_general(weighted, gathered, (((1,), (1,)), ((), ())), preferred_e...  7.53 us
    unnamed x9, local copies, waits for them, and re-layouts  6.09 us
  transfers between devices with their start and end apart: 2, of which 1 were waited for; matrix products, arithmetic and copies ran while one was open for 5% of the time, Pallas kernels for 46%

profile of v3, /device:TPU:12, one launch (start us, length us, event | category | flops | bytes accessed | tf_op | source)
XLA Modules:
  0.0 266.6 jit_solution(11753627002045432675)
XLA Ops:
  7.2 0.0 all-gather.8.cloned.1.call-start
  7.2 0.7 all-gather.8.cloned.1.call-update
  7.9 0.0 all-gather.6.cloned.1.call-start
  7.9 1.0 copy.20
  9.0 1.0 copy.19
  10.0 1.9 copy.24
  11.9 1.0 copy.25
  12.9 0.8 reshape.36.idx_ref
  13.7 0.7 pad_maximum_fusion
  14.4 5.7 %fusion.2 = f32[256]{0:T(256)S(1)} fusion(bf16[256,16384]{1,0:T(8,128)(2,1)} %param.6, f32[16384]{0:T(1024)} %bitcast.31), kind=kLoop, calls=%fused_computation.4 | loop fusion | flops 16776960 | bytes 8455168 | tf_op jit(solution)/shard_map/reduce_sum | solution.py:310
  20.1 0.0 copy-start.1
  20.1 64.6 %all-gather.8.cloned.1.call-done = bf16[16,12,16384]{2,1,0:T(8,128)(2,1)} async-done(((bf16[1,12,16384]{2,1,0:T(8,128)(2,1)}), bf16[16,12,16384]{2,1,0:T(8,128)(2,1)}) %all-gather.8.cloned.1.call-update) | async-done | bytes 6291472 | tf_op jit(solution)/shard_map/all_gather | solution.py:304
  84.7 8.8 %reshape.42.images_ref = bf16[192,16384]{1,0:T(8,128)(2,1)} reshape(bf16[16,12,16384]{2,1,0:T(8,128)(2,1)} %all-gather.8.cloned.1.call-done) | data formatting | bytes 12582912 | tf_op jit(solution)/shard_map/optimization_barrier | solution.py:306
  93.5 0.0 copy-done.1
  93.5 7.5 %fusion.16 = (f32[192]{0:T(256)S(1)}, f32[256,192]{1,0:T(8,128)S(1)}) fusion(f32[256]{0:T(256)S(1)} %broadcast_multiply_fusion, bf16[192,16384]{1,0:T(8,128)(2,1)} %reshape.42.images_ref, bf16[256,16384]{1,0:T(8,128)(2,1)} %param.6, f32[16384]{0:T(1024)S(1)} %bitcast.32), kind=kOutput, calls=%fused_computation.27 | convolution fusion | flops 1623293696 | bytes 14944000 | tf_op jit(solution)/shard_map/dot_general | solution.py:312
  101.0 0.1 fusion.12
  101.1 16.5 %all-gather.2 = f32[16,2,192]{2,1,0:T(2,128)S(1)} all-gather(f32[1,2,192]{2,1,0:T(2,128)S(1)} %maximum_bitcast_fusion), channel_id=2, replica_groups=mesh['dp'=2,'orient'=16] {'orient'}, dimensions={0}, use_global_device_ids=true | all-gather | bytes 26112 | tf_op jit(solution)/shard_map/all_gather | solution.py:319
  117.7 0.7 multiply_reduce_fusion
  118.4 0.0 all-gather.6.cloned.1.call-update
  118.4 64.7 %shard_map.68 = f32[16384,128]{1,0:T(8,128)} custom-call(bf16[256,192]{1,0:T(8,128)(2,1)} %get-tuple-element.11.post_ref, bf16[192,16384]{1,0:T(8,128)(2,1)} %reshape.42.images_ref, f32[16,256,8]{2,1,0:T(8,128)} %bitcast.34, s32[16,1,2048]{2,1,0:T(1,128)} %reshape.36.idx_ref), custom_call_target="tpu_custom_call" | custom-call | flops 199999995904 | bytes 200000000 | tf_op jit(solution)/shard_map/pallas_call | solution.py:66
  183.2 0.0 copy-start
  183.2 3.4 %copy-done = f32[16384,128]{1,0:T(8,128)S(1)} copy-done((f32[16384,128]{1,0:T(8,128)S(1)}, f32[16384,128]{1,0:T(8,128)}, u32[]{:S(2)}) %copy-start) | copy-done | bytes 8388632
  186.6 56.6 %shard_map.69 = (f32[512,128]{1,0:T(8,128)S(1)}, f32[32,2,128]{2,1,0:T(2,128)S(1)}) custom-call(f32[16,2,512,128]{3,2,1,0:T(8,128)S(1)} %bitcast.30, f32[2,128]{1,0:T(2,128)S(1)} %bitcast.33), custom_call_target="tpu_custom_call" | custom-call | tf_op jit(solution)/shard_map/pallas_call | solution.py:214
  243.2 0.0 copy-start.2
  243.3 0.0 all-gather.6.cloned.1.call-done
  243.3 1.8 fusion.6.weight_ref
  245.1 1.8 fusion.8.local_ref
  247.0 0.0 copy-done.2
  247.0 12.0 %shard_map.70 = f32[512,128]{1,0:T(8,128)} custom-call(s32[128,4096]{1,0:T(8,128)S(1)} %fusion.8.local_ref, f32[128,4096]{1,0:T(8,128)S(1)} %fusion.6.weight_ref, f32[128,128]{1,0:T(8,128)S(1)} %copy-done.2), custom_call_target="tpu_custom_call" | custom-call | flops 60000002048 | bytes 20000000 | tf_op jit(solution)/shard_map/pallas_call | solution.py:281
  259.0 0.7 copy.36
  (8 shorter events, 0.2 us)
Async XLA Ops:
  7.2 77.5 %all-gather.8.cloned.1.call-start = ((), (), s32[]{:S(2)}) async-start(), calls=%async_computation.1 | async-start | bytes 8912896 | tf_op jit(solution)/shard_map/all_gather | solution.py:304
  7.9 235.4 %all-gather.6.cloned.1.call-start = ((), (), s32[]{:S(2)}) async-start(), calls=%async_computation | async-start | bytes 4456448 | tf_op jit(solution)/shard_map/all_gather | solution.py:307
  20.1 73.4 %copy-start.1 = (f32[128,128]{1,0:T(8,128)S(1)}, f32[128,128]{1,0:T(8,128)}, u32[]{:S(2)}) copy-start(f32[128,128]{1,0:T(8,128)} %noise_ref.1) | copy-start | bytes 196612
  183.2 3.4 %copy-start = (f32[16384,128]{1,0:T(8,128)S(1)}, f32[16384,128]{1,0:T(8,128)}, u32[]{:S(2)}) copy-start(f32[16384,128]{1,0:T(8,128)} %shard_map.68) | copy-start | bytes 25165828
  243.2 3.8 %copy-start.2 = (f32[128,128]{1,0:T(8,128)S(1)}, f32[128,128]{1,0:T(8,128)}, u32[]{:S(2)}) copy-start(f32[128,128]{1,0:T(8,128)} %noise_ref.1) | copy-start | bytes 196612
Sparse Core Ops, SparseCore 0:
  10.2 74.4 all-gather.7
  118.6 51.4 all-gather.5

commit v4 on v3

--- a/solution.py
+++ b/solution.py
@@ -41,10 +41,14 @@
     @pl.loop(0, ROWS_STEP * count // UNROLL)
     def _(g):
         base = pl.multiple_of(g * UNROLL, UNROLL)
-        for k in range(UNROLL):
-            acc = accs[k % ACCS]
-            v = idx_ref[0, 0, base + k]
-            acc[pl.ds(v, 1), :] += rows_ref[pl.ds(base + k, 1), :]
+        for k in range(0, UNROLL, ACCS):
+            voxels = [idx_ref[0, 0, base + k + a] for a in range(ACCS)]
+            summed = [
+                accs[a][pl.ds(voxels[a], 1), :] + rows_ref[pl.ds(base + k + a, 1), :]
+                for a in range(ACCS)
+            ]
+            for a in range(ACCS):
+                accs[a][pl.ds(voxels[a], 1), :] = summed[a]
 
     @pl.when(step == pl.num_programs(0) - 1)
     def _():
@@ -231,7 +235,7 @@
         + [pltpu.SemaphoreType.DMA((chips,))] * 5
         + [pltpu.SemaphoreType.DMA((2 * chips,))] * 2,
         compiler_params=pltpu.CompilerParams(
-            collective_id=0, has_side_effects=True, vmem_limit_bytes=32 * 2**20
+            collective_id=0, has_side_effects=True, vmem_limit_bytes=VMEM_LIMIT
         ),
     )(volume.reshape(chips, 2, rows, side), mass_rows)
 
@@ -296,6 +300,62 @@
     )(local_t, weight_t, inv_noise)
 
 
+def stats_kernel(orient, own_ref, out_ref, landed, send_sem, recv_sem):
+    group, place = lax.axis_index("dp"), lax.axis_index("orient")
+    mesh_ids = pl.DeviceIdType.MESH
+    barrier = pltpu.get_barrier_semaphore()
+
+    @pl.loop(1, orient)
+    def _(s):
+        pl.semaphore_signal(
+            barrier,
+            inc=1,
+            device_id=(group, lax.rem(place + s, orient)),
+            device_id_type=mesh_ids,
+        )
+
+    pl.semaphore_wait(barrier, orient - 1)
+
+    def copy(s):
+        return pltpu.make_async_remote_copy(
+            src_ref=own_ref,
+            dst_ref=landed.at[s],
+            send_sem=send_sem.at[s],
+            recv_sem=recv_sem.at[s],
+            device_id=(group, lax.rem(place + s, orient)),
+            device_id_type=mesh_ids,
+        )
+
+    @pl.loop(1, orient)
+    def _(s):
+        copy(s).start()
+
+    out_ref[place] = own_ref[...]
+
+    @pl.loop(1, orient)
+    def _(s):
+        copy(s).wait()
+        out_ref[lax.rem(place + orient - s, orient)] = landed[s]
+
+
+def gather_stats(own, orient):
+    count = own.shape[1]
+    pad = -count % (8 * LANES)
+    rows = jnp.pad(own, ((0, 0), (0, pad))).reshape(-1, LANES)
+    stats = pl.pallas_call(
+        functools.partial(stats_kernel, orient),
+        out_shape=jax.ShapeDtypeStruct((orient,) + rows.shape, jnp.float32),
+        in_specs=[pl.BlockSpec(memory_space=pltpu.VMEM)],
+        out_specs=pl.BlockSpec(memory_space=pltpu.VMEM),
+        scratch_shapes=[pltpu.VMEM((orient,) + rows.shape, jnp.float32)]
+        + [pltpu.SemaphoreType.DMA((orient,))] * 2,
+        compiler_params=pltpu.CompilerParams(
+            collective_id=1, has_side_effects=True, vmem_limit_bytes=16 * 2**20
+        ),
+    )(rows)
+    return stats.reshape(orient, 2, -1)[:, :, :count]
+
+
 def shards(groups, orient, images, templates, index, interp, inv_noise):
     side = inv_noise.shape[0]
     volume_rows = side * side
@@ -316,7 +376,7 @@
     )
     peak_own = jnp.max(scores, axis=0)
     expo = jnp.exp(scores - peak_own[None, :])
-    stats = lax.all_gather(jnp.stack([peak_own, jnp.sum(expo, axis=0)]), "orient", axis=0)
+    stats = gather_stats(jnp.stack([peak_own, jnp.sum(expo, axis=0)]), orient)
     peak = jnp.max(stats[:, 0], axis=0)
     total = jnp.sum(stats[:, 1] * jnp.exp(stats[:, 0] - peak[None, :]), axis=0)
     posterior = expo * (jnp.exp(peak_own - peak) / total)[None, :]

time: 267 us -> 253 us (0.948)
  blocking collectives: 16.5 us -> 0 us
  Pallas kernels: 133 us -> 138 us
    all_gather x1 -> x0, blocking collectives: 16.5 us -> none  [shards(): lax.all_gather(jnp.stack([peak_own, jnp.sum(expo, axis=0)]), 'orient', ax...]
    pallas_call x0 -> x1, Pallas kernels: none -> 7.64 us  [gather_stats(): pl.pallas_call(functools.partial(stats_kernel, orient), out_shape=jax.Sha...]
    unnamed x9, local copies, waits for them, and re-layouts: 6.09 us -> 2.72 us
  transfers between devices with their start and end apart: 2 -> 2, of which waited for: 1 -> 1; matrix products, arithmetic and copies ran while one was open for 5% -> 5% of each run, Pallas kernels for 46% -> 47%
where the time goes in v4:
time: 253 us
  Pallas kernels  138 us (55%)
  waiting for transfers between devices  65.3 us (26%)
  local copies, waits for them, and re-layouts  16.1 us (6%)
  between operations  14.2 us (6%)
  other arithmetic  11.5 us (5%)
  matrix products  7.53 us (3%)
    all_gather x1, waiting for transfers between devices, shards(): gathered = lax.all_gather(images, 'orient', axis=0, tiled=True)  64.6 us
    pallas_call x1, Pallas kernels, insert_data(): pl.pallas_call(data_kernel, grid=(steps,), out_shape=jax.ShapeDtypeStruct...  62.6 us
    pallas_call x1, Pallas kernels, reduce_rows(): pl.pallas_call(functools.partial(reduce_kernel, groups, orient), out_shap...  55.7 us
    pallas_call x1, Pallas kernels, own_weights(): pl.pallas_call(weight_kernel, grid=(side // ROWS_STEP,), out_shape=jax.Sh...  12 us
    optimization_barrier x1, local copies, waits for them, and re-layouts, shards(): gathered, places = lax.optimization_barrier((gathered, places))  8.78 us
    pallas_call x1, Pallas kernels, gather_stats(): pl.pallas_call(functools.partial(stats_kernel, orient), out_shape=jax.Sha...  7.64 us
    dot_general x1, matrix products, shards(): lax.dot_general(weighted, gathered, (((1,), (1,)), ((), ())), preferred_e...  7.53 us
    reduce_sum x1, other arithmetic, shards(): tnorm = 0.5 * jnp.sum(tpl_f * tpl_f * noise_flat[None, :], axis=1)  5.67 us
  transfers between devices with their start and end apart: 2, of which 1 were waited for; matrix products, arithmetic and copies ran while one was open for 5% of the time, Pallas kernels for 47%

profile of v4, /device:TPU:12, one launch (start us, length us, event | category | flops | bytes accessed | tf_op | source)
XLA Modules:
  0.0 252.7 jit_solution(13844075822610518893)
XLA Ops:
  7.2 0.0 all-gather.6.cloned.1.call-start
  7.2 0.7 all-gather.6.cloned.1.call-update
  7.9 0.0 all-gather.4.cloned.1.call-start
  7.9 1.0 copy.20
  9.0 1.0 copy.19
  10.0 1.9 copy.24
  11.9 1.0 copy.25
  12.9 0.8 reshape.44.idx_ref
  13.7 0.7 pad_maximum_fusion
  14.4 5.7 %fusion.2 = f32[256]{0:T(256)S(1)} fusion(bf16[256,16384]{1,0:T(8,128)(2,1)} %param.6, f32[16384]{0:T(1024)} %bitcast.28), kind=kLoop, calls=%fused_computation.4 | loop fusion | flops 16776960 | bytes 8455168 | tf_op jit(solution)/shard_map/reduce_sum | solution.py:370
  20.1 0.0 copy-start
  20.1 64.6 %all-gather.6.cloned.1.call-done = bf16[16,12,16384]{2,1,0:T(8,128)(2,1)} async-done(((bf16[1,12,16384]{2,1,0:T(8,128)(2,1)}), bf16[16,12,16384]{2,1,0:T(8,128)(2,1)}) %all-gather.6.cloned.1.call-update) | async-done | bytes 6291472 | tf_op jit(solution)/shard_map/all_gather | solution.py:364
  84.7 8.8 %reshape.49.images_ref = bf16[192,16384]{1,0:T(8,128)(2,1)} reshape(bf16[16,12,16384]{2,1,0:T(8,128)(2,1)} %all-gather.6.cloned.1.call-done) | data formatting | bytes 12582912 | tf_op jit(solution)/shard_map/optimization_barrier | solution.py:366
  93.5 0.0 copy-done
  93.5 7.5 %fusion.17 = (f32[192]{0:T(256)S(1)}, f32[256,192]{1,0:T(8,128)S(1)}) fusion(f32[256]{0:T(256)S(1)} %broadcast_multiply_fusion, bf16[192,16384]{1,0:T(8,128)(2,1)} %reshape.49.images_ref, bf16[256,16384]{1,0:T(8,128)(2,1)} %param.6, f32[16384]{0:T(1024)S(1)} %bitcast.29), kind=kOutput, calls=%fused_computation.27 | convolution fusion | flops 1623293696 | bytes 14944000 | tf_op jit(solution)/shard_map/dot_general | solution.py:372
  101.0 0.1 fusion.12
  101.1 7.6 %shard_map.68 = f32[16,16,128]{2,1,0:T(8,128)S(1)} custom-call(f32[16,128]{1,0:T(8,128)S(1)} %reshape.41.own_ref), custom_call_target="tpu_custom_call" | custom-call | tf_op jit(solution)/shard_map/pallas_call | solution.py:345
  108.8 0.1 reshape.42
  108.9 1.3 multiply_reduce_fusion
  110.2 0.0 all-gather.4.cloned.1.call-update
  110.2 62.6 %shard_map.69 = f32[16384,128]{1,0:T(8,128)} custom-call(bf16[256,192]{1,0:T(8,128)(2,1)} %get-tuple-element.11.post_ref, bf16[192,16384]{1,0:T(8,128)(2,1)} %reshape.49.images_ref, f32[16,256,8]{2,1,0:T(8,128)} %bitcast.31, s32[16,1,2048]{2,1,0:T(1,128)} %reshape.44.idx_ref), custom_call_target="tpu_custom_call" | custom-call | flops 199999995904 | bytes 200000000 | tf_op jit(solution)/shard_map/pallas_call | solution.py:70
  172.8 55.7 %shard_map.70 = (f32[512,128]{1,0:T(8,128)}, f32[32,2,128]{2,1,0:T(2,128)}) custom-call(f32[16,2,512,128]{3,2,1,0:T(8,128)} %bitcast.30, f32[2,128]{1,0:T(2,128)} %bitcast.36), custom_call_target="tpu_custom_call" | custom-call | tf_op jit(solution)/shard_map/pallas_call | solution.py:218
  228.5 0.0 copy-start.1
  228.5 0.8 reshape.47
  229.4 0.0 all-gather.4.cloned.1.call-done
  229.5 1.8 fusion.6.weight_ref
  231.3 1.8 fusion.8.local_ref
  233.1 0.0 copy-done.1
  233.1 0.0 copy-start.2
  233.1 12.0 %shard_map.71 = f32[512,128]{1,0:T(8,128)} custom-call(s32[128,4096]{1,0:T(8,128)S(1)} %fusion.8.local_ref, f32[128,4096]{1,0:T(8,128)S(1)} %fusion.6.weight_ref, f32[128,128]{1,0:T(8,128)S(1)} %copy-done.1), custom_call_target="tpu_custom_call" | custom-call | flops 60000002048 | bytes 20000000 | tf_op jit(solution)/shard_map/pallas_call | solution.py:285
  245.2 0.0 copy-done.2
  245.2 0.7 copy.41
  (8 shorter events, 0.2 us)
Async XLA Ops:
  7.2 77.5 %all-gather.6.cloned.1.call-start = ((), (), s32[]{:S(2)}) async-start(), calls=%async_computation.1 | async-start | bytes 8912896 | tf_op jit(solution)/shard_map/all_gather | solution.py:364
  7.9 221.5 %all-gather.4.cloned.1.call-start = ((), (), s32[]{:S(2)}) async-start(), calls=%async_computation | async-start | bytes 4456448 | tf_op jit(solution)/shard_map/all_gather | solution.py:367
  20.1 73.4 %copy-start = (f32[128,128]{1,0:T(8,128)S(1)}, f32[128,128]{1,0:T(8,128)}, u32[]{:S(2)}) copy-start(f32[128,128]{1,0:T(8,128)} %noise_ref.1) | copy-start | bytes 196612
  228.5 4.6 %copy-start.1 = (f32[128,128]{1,0:T(8,128)S(1)}, f32[128,128]{1,0:T(8,128)}, u32[]{:S(2)}) copy-start(f32[128,128]{1,0:T(8,128)} %noise_ref.1) | copy-start | bytes 196612
  233.1 12.1 %copy-start.2 = (f32[512,128]{1,0:T(8,128)S(1)}, f32[512,128]{1,0:T(8,128)}, u32[]{:S(2)}) copy-start(f32[512,128]{1,0:T(8,128)} %get-tuple-element.19) | copy-start | bytes 786436
Sparse Core Ops, SparseCore 0:
  10.2 74.4 all-gather.5
  110.4 50.8 all-gather.3

commit v5 on v4

--- a/solution.py
+++ b/solution.py
@@ -96,8 +96,13 @@
     orient,
     blocks_ref,
     mass_ref,
+    local_ref,
+    interp_ref,
+    noise_ref,
     out_ref,
-    masses_ref,
+    weight_ref,
+    grid_ref,
+    mass_row,
     mine,
     theirs,
     ready,
@@ -176,16 +181,16 @@
             device_id_type=mesh_ids,
         )
 
+    @pl.loop(1, devices)
+    def _(s):
+        mass_copy(s).start()
+
     @pl.loop(1, chips + 1)
     def _(k):
         s = lax.rem(k, chips)
         own_copy(s).start()
         pair_copy(s).start()
 
-    @pl.loop(1, devices)
-    def _(s):
-        mass_copy(s).start()
-
     @pl.loop(1, chips)
     def _(s):
         own_copy(s).wait()
@@ -196,12 +201,23 @@
     own_copy(0).wait()
     pair_copy(0).wait()
     out_ref[...] = mine[0] + theirs[0]
-    masses_ref[rank] = mass_ref[...]
+    mass_row[...] = jnp.zeros_like(mass_row)
+    mass_rows = mass_ref.shape[0]
+
+    def add_mass(d, ref):
+        start = lax.rem(d, orient) * (mass_rows * LANES)
+        for k in range(mass_rows):
+            lanes = pl.ds(pl.multiple_of(start + k * LANES, LANES), LANES)
+            mass_row[:, lanes] += ref[k : k + 1, :]
+
+    add_mass(rank, mass_ref)
 
     @pl.loop(1, devices)
     def _(s):
         mass_copy(s).wait()
-        masses_ref[lax.rem(rank + devices - s, devices)] = masses[s]
+        add_mass(lax.rem(rank + devices - s, devices), masses.at[s])
+
+    insert_weights(local_ref, interp_ref, mass_row, noise_ref, weight_ref, grid_ref)
 
     @pl.loop(1, chips)
     def _(s):
@@ -209,7 +225,7 @@
         out_ref[...] += landed[s].astype(jnp.float32)
 
 
-def reduce_rows(volume, mass, groups, orient):
+def reduce_rows(volume, mass, local_t, interp_t, inv_noise, groups, orient):
     chips = groups * orient // 2
     rows, side = volume.shape[0] // (2 * chips), volume.shape[1]
     parts = (chips, rows, side)
@@ -219,17 +235,19 @@
         functools.partial(reduce_kernel, groups, orient),
         out_shape=(
             jax.ShapeDtypeStruct((rows, side), jnp.float32),
-            jax.ShapeDtypeStruct(masses, jnp.float32),
-        ),
-        in_specs=[
-            pl.BlockSpec(memory_space=pl.ANY),
-            pl.BlockSpec(memory_space=pltpu.VMEM),
-        ],
+            jax.ShapeDtypeStruct((rows, side), jnp.float32),
+        ),
+        in_specs=[pl.BlockSpec(memory_space=pl.ANY)]
+        + [pl.BlockSpec(memory_space=pltpu.VMEM)] * 4,
         out_specs=(
             pl.BlockSpec(memory_space=pltpu.VMEM),
             pl.BlockSpec(memory_space=pltpu.VMEM),
         ),
-        scratch_shapes=[pltpu.VMEM(parts, jnp.float32)] * 2
+        scratch_shapes=[
+            pltpu.VMEM((side * max(8, rows // LOW), LANES), jnp.float32),
+            pltpu.VMEM((1, local_t.shape[1]), jnp.float32),
+        ]
+        + [pltpu.VMEM(parts, jnp.float32)] * 2
         + [pltpu.VMEM(parts, jnp.bfloat16)] * 2
         + [pltpu.VMEM(masses, jnp.float32)]
         + [pltpu.SemaphoreType.DMA((chips,))] * 5
@@ -237,7 +255,7 @@
         compiler_params=pltpu.CompilerParams(
             collective_id=0, has_side_effects=True, vmem_limit_bytes=VMEM_LIMIT
         ),
-    )(volume.reshape(chips, 2, rows, side), mass_rows)
+    )(volume.reshape(chips, 2, rows, side), mass_rows, local_t, interp_t, inv_noise)
 
 
 def split(value):
@@ -245,59 +263,40 @@
     return high, (value - high.astype(jnp.float32)).astype(jnp.bfloat16)
 
 
-def weight_kernel(local_ref, weight_ref, noise_ref, out_ref, grid_ref):
-    step = pl.program_id(0)
+def insert_weights(local_ref, interp_ref, mass_row, noise_ref, out_ref, grid_ref):
     count = local_ref.shape[1]
     side = noise_ref.shape[0]
     high_rows = grid_ref.shape[0] // side
     nt = (((1,), (1,)), ((), ()))
-    iota_high = lax.broadcasted_iota(jnp.int32, (high_rows, count), 0)
-    iota_low = lax.broadcasted_iota(jnp.int32, (LOW, count), 0)
+    tn = (((0,), (0,)), ((), ()))
     one, zero = jnp.float32(1), jnp.float32(0)
-    for j in range(ROWS_STEP):
-        local = local_ref[j : j + 1, :]
-        hot = jnp.where(iota_high == (local >> LOW_BITS), one, zero)
-        low = jnp.where(iota_low == (local & (LOW - 1)), weight_ref[j : j + 1, :], zero)
-        part = lax.dot_general(
-            hot.astype(jnp.bfloat16),
-            low.astype(jnp.bfloat16),
-            nt,
-            preferred_element_type=jnp.float32,
-        )
-        row = pl.multiple_of((step * ROWS_STEP + j) * high_rows, 8)
-        grid_ref[pl.ds(row, high_rows), :LOW] = part
-
-    @pl.when(step == pl.num_programs(0) - 1)
-    def _():
-        noise = noise_ref[...].astype(jnp.bfloat16)
-        tn = (((0,), (0,)), ((), ()))
-        for h in range(out_ref.shape[0] // LOW):
-            high, low = split(grid_ref[pl.ds(h, side, stride=high_rows), :])
-            block = lax.dot_general(
-                high, noise, tn, preferred_element_type=jnp.float32
-            ) + lax.dot_general(low, noise, tn, preferred_element_type=jnp.float32)
-            out_ref[h * LOW : (h + 1) * LOW, :] = block[:LOW]
-
-
-def own_weights(local_t, weight_t, inv_noise, rows):
-    side, count = local_t.shape
-    high_rows = max(8, rows // LOW)
-    return pl.pallas_call(
-        weight_kernel,
-        grid=(side // ROWS_STEP,),
-        out_shape=jax.ShapeDtypeStruct((rows, side), jnp.float32),
-        in_specs=[
-            pl.BlockSpec((ROWS_STEP, count), lambda i: (i, 0)),
-            pl.BlockSpec((ROWS_STEP, count), lambda i: (i, 0)),
-            pl.BlockSpec((side, side), lambda i: (0, 0)),
-        ],
-        out_specs=pl.BlockSpec((rows, side), lambda i: (0, 0)),
-        scratch_shapes=[pltpu.VMEM((side * high_rows, LANES), jnp.float32)],
-        compiler_params=pltpu.CompilerParams(vmem_limit_bytes=24 * 2**20),
-        cost_estimate=pl.CostEstimate(
-            flops=60_000_000_000, bytes_accessed=20_000_000, transcendentals=0
-        ),
-    )(local_t, weight_t, inv_noise)
+
+    @pl.loop(0, side // ROWS_STEP)
+    def _(step):
+        iota_high = lax.broadcasted_iota(jnp.int32, (high_rows, count), 0)
+        iota_low = lax.broadcasted_iota(jnp.int32, (LOW, count), 0)
+        block = pl.ds(pl.multiple_of(step * ROWS_STEP, ROWS_STEP), ROWS_STEP)
+        locals_, weights = local_ref[block, :], interp_ref[block, :] * mass_row[...]
+        for j in range(ROWS_STEP):
+            local = locals_[j : j + 1, :]
+            hot = jnp.where(iota_high == (local >> LOW_BITS), one, zero)
+            low = jnp.where(iota_low == (local & (LOW - 1)), weights[j : j + 1, :], zero)
+            part = lax.dot_general(
+                hot.astype(jnp.bfloat16),
+                low.astype(jnp.bfloat16),
+                nt,
+                preferred_element_type=jnp.float32,
+            )
+            row = pl.multiple_of((step * ROWS_STEP + j) * high_rows, 8)
+            grid_ref[pl.ds(row, high_rows), :LOW] = part
+
+    noise = noise_ref[...].astype(jnp.bfloat16)
+    for h in range(out_ref.shape[0] // LOW):
+        high, low = split(grid_ref[pl.ds(h, side, stride=high_rows), :])
+        block = lax.dot_general(
+            high, noise, tn, preferred_element_type=jnp.float32
+        ) + lax.dot_general(low, noise, tn, preferred_element_type=jnp.float32)
+        out_ref[h * LOW : (h + 1) * LOW, :] = block[:LOW]
 
 
 def stats_kernel(orient, own_ref, out_ref, landed, send_sem, recv_sem):
@@ -386,15 +385,15 @@
     )
     rows = volume_rows // (groups * orient)
     first = (lax.axis_index("dp") * orient + lax.axis_index("orient")) * rows
-    data_own, masses = reduce_rows(data_vol, mass, groups, orient)
-    mass_all = jnp.sum(masses.reshape(groups, -1), axis=0)
-    weight_own = own_weights(
+    return reduce_rows(
+        data_vol,
+        mass,
         places_all[:, :side].astype(jnp.int32).T - first,
-        places_all[:, side:].T * mass_all[None, :],
+        places_all[:, side:].T,
         inv_noise,
-        rows,
+        groups,
+        orient,
     )
-    return data_own, weight_own
 
 
 def solution(mesh):

time: 253 us -> 247 us (0.976)
  Pallas kernels: 138 us -> 128 us
  local copies, waits for them, and re-layouts: 16.1 us -> 21 us
    pallas_call x1 -> x0, Pallas kernels: 12 us -> none  [own_weights(): pl.pallas_call(weight_kernel, grid=(side // ROWS_STEP,), out_shape=jax.Sh...]
    transpose x0 -> x1, local copies, waits for them, and re-layouts: none -> 3.09 us  [shards(): places_all[:, side:]]
    unnamed x9 -> x6, local copies, waits for them, and re-layouts: 2.72 us -> 5.34 us
  transfers between devices with their start and end apart: 2 -> 2, of which waited for: 1 -> 1; matrix products, arithmetic and copies ran while one was open for 5% -> 5% of each run, Pallas kernels for 47% -> 25%
where the time goes in v5:
time: 247 us
  Pallas kernels  128 us (52%)
  waiting for transfers between devices  65.3 us (26%)
  local copies, waits for them, and re-layouts  21 us (9%)
  between operations  14.1 us (6%)
  other arithmetic  11.1 us (4%)
  matrix products  7.53 us (3%)
    all_gather x1, waiting for transfers between devices, shards(): gathered = lax.all_gather(images, 'orient', axis=0, tiled=True)  64.6 us
    pallas_call x1, Pallas kernels, insert_data(): pl.pallas_call(data_kernel, grid=(steps,), out_shape=jax.ShapeDtypeStruct...  62.6 us
    pallas_call x1, Pallas kernels, reduce_rows(): pl.pallas_call(functools.partial(reduce_kernel, groups, orient), out_shap...  57.6 us
    optimization_barrier x1, local copies, waits for them, and re-layouts, shards(): gathered, places = lax.optimization_barrier((gathered, places))  8.78 us
    pallas_call x1, Pallas kernels, gather_stats(): pl.pallas_call(functools.partial(stats_kernel, orient), out_shape=jax.Sha...  7.64 us
    dot_general x1, matrix products, shards(): lax.dot_general(weighted, gathered, (((1,), (1,)), ((), ())), preferred_e...  7.53 us
    reduce_sum x1, other arithmetic, shards(): tnorm = 0.5 * jnp.sum(tpl_f * tpl_f * noise_flat[None, :], axis=1)  5.67 us
    unnamed x6, local copies, waits for them, and re-layouts  5.34 us
  transfers between devices with their start and end apart: 2, of which 1 were waited for; matrix products, arithmetic and copies ran while one was open for 5% of the time, Pallas kernels for 25%

profile of v5, /device:TPU:12, one launch (start us, length us, event | category | flops | bytes accessed | tf_op | source)
XLA Modules:
  0.0 246.9 jit_solution(15471030464590966468)
XLA Ops:
  7.2 0.0 all-gather.6.cloned.1.call-start
  7.2 0.7 all-gather.6.cloned.1.call-update
  7.9 0.0 all-gather.4.cloned.1.call-start
  7.9 1.0 copy.20
  9.0 1.0 copy.19
  10.0 1.9 copy.24
  11.9 1.0 copy.25
  12.9 0.8 reshape.40.idx_ref
  13.7 0.7 pad_maximum_fusion
  14.4 5.7 %fusion.2 = f32[256]{0:T(256)S(1)} fusion(bf16[256,16384]{1,0:T(8,128)(2,1)} %param.6, f32[16384]{0:T(1024)} %bitcast.33), kind=kLoop, calls=%fused_computation.4 | loop fusion | flops 16776960 | bytes 8455168 | tf_op jit(solution)/shard_map/reduce_sum | solution.py:369
  20.1 0.0 copy-start
  20.1 64.6 %all-gather.6.cloned.1.call-done = bf16[16,12,16384]{2,1,0:T(8,128)(2,1)} async-done(((bf16[1,12,16384]{2,1,0:T(8,128)(2,1)}), bf16[16,12,16384]{2,1,0:T(8,128)(2,1)}) %all-gather.6.cloned.1.call-update) | async-done | bytes 6291472 | tf_op jit(solution)/shard_map/all_gather | solution.py:363
  84.7 8.8 %reshape.44.images_ref = bf16[192,16384]{1,0:T(8,128)(2,1)} reshape(bf16[16,12,16384]{2,1,0:T(8,128)(2,1)} %all-gather.6.cloned.1.call-done) | data formatting | bytes 12582912 | tf_op jit(solution)/shard_map/optimization_barrier | solution.py:365
  93.5 0.0 copy-done
  93.5 7.5 %fusion.16 = (f32[192]{0:T(256)S(1)}, f32[256,192]{1,0:T(8,128)S(1)}) fusion(f32[256]{0:T(256)S(1)} %broadcast_multiply_fusion, bf16[192,16384]{1,0:T(8,128)(2,1)} %reshape.44.images_ref, bf16[256,16384]{1,0:T(8,128)(2,1)} %param.6, f32[16384]{0:T(1024)S(1)} %bitcast.34), kind=kOutput, calls=%fused_computation.26 | convolution fusion | flops 1623293696 | bytes 14944000 | tf_op jit(solution)/shard_map/dot_general | solution.py:371
  101.0 0.1 fusion.11
  101.1 7.6 %shard_map.68 = f32[16,16,128]{2,1,0:T(8,128)S(1)} custom-call(f32[16,128]{1,0:T(8,128)S(1)} %reshape.37.own_ref), custom_call_target="tpu_custom_call" | custom-call | tf_op jit(solution)/shard_map/pallas_call | solution.py:344
  108.8 0.1 reshape.38
  108.9 1.3 multiply_reduce_fusion
  110.2 0.0 all-gather.4.cloned.1.call-update
  110.2 62.6 %shard_map.69 = f32[16384,128]{1,0:T(8,128)} custom-call(bf16[256,192]{1,0:T(8,128)(2,1)} %get-tuple-element.7.post_ref, bf16[192,16384]{1,0:T(8,128)(2,1)} %reshape.44.images_ref, f32[16,256,8]{2,1,0:T(8,128)} %bitcast.29, s32[16,1,2048]{2,1,0:T(1,128)} %reshape.40.idx_ref), custom_call_target="tpu_custom_call" | custom-call | flops 199999995904 | bytes 200000000 | tf_op jit(solution)/shard_map/pallas_call | solution.py:70
  172.8 0.0 all-gather.4.cloned.1.call-done
  172.8 3.1 %slice_bitcast_fusion.interp_ref = f32[128,4096]{1,0:T(8,128)} fusion(f32[4096,256]{0,1:T(8,128)} %all-gather.4.cloned.1.call-done), kind=kLoop, calls=%fused_computation.7 | loop fusion | bytes 4194304 | tf_op jit(solution)/shard_map/transpose | solution.py:392
  175.9 3.2 %fusion.7.local_ref = s32[128,4096]{1,0:T(8,128)} fusion(f32[4096,256]{0,1:T(8,128)} %all-gather.4.cloned.1.call-done, s32[]{:T(128)S(6)} %mul.57), kind=kLoop, calls=%fused_computation.10 | loop fusion | flops 1048576 | bytes 4194308 | tf_op jit(solution)/shard_map/sub | solution.py:391
  179.1 57.6 %shard_map.70 = (f32[512,128]{1,0:T(8,128)}, f32[512,128]{1,0:T(8,128)}) custom-call(f32[16,2,512,128]{3,2,1,0:T(8,128)} %bitcast.28, f32[2,128]{1,0:T(2,128)} %bitcast.36, s32[128,4096]{1,0:T(8,128)} %fusion.7.local_ref, f32[128,4096]{1,0:T(8,128)} %slice_bitcast_fusion.interp_ref, f32[128,128]{1,0:T(8,128)} %noise_ref.1), custom_call_target="tpu_custom_call" | custom-call | tf_op jit(solution)/shard_map/pallas_call | solution.py:234
  236.7 1.7 copy.42
  238.4 1.7 copy.43
  (7 shorter events, 0.1 us)
Async XLA Ops:
  7.2 77.5 %all-gather.6.cloned.1.call-start = ((), (), s32[]{:S(2)}) async-start(), calls=%async_computation.1 | async-start | bytes 8912896 | tf_op jit(solution)/shard_map/all_gather | solution.py:363
  7.9 164.9 %all-gather.4.cloned.1.call-start = ((), (), s32[]{:S(2)}) async-start(), calls=%async_computation | async-start | bytes 4456448 | tf_op jit(solution)/shard_map/all_gather | solution.py:366
  20.1 73.4 %copy-start = (f32[128,128]{1,0:T(8,128)S(1)}, f32[128,128]{1,0:T(8,128)}, u32[]{:S(2)}) copy-start(f32[128,128]{1,0:T(8,128)} %noise_ref.1) | copy-start | bytes 196612
Sparse Core Ops, SparseCore 0:
  10.2 74.4 all-gather.5
  110.4 50.8 all-gather.3
